TPU v7x, 32 devices: a whole 2x2x4 slice. The times are simulated.
32 devices in a mesh: space: 8 (over z, y), sub: 4 (over x, core).
Axes of the slice: x: 2, y: 2, z: 4, core: 2. Of those that a mesh axis runs over, the one named last changes fastest.
Arguments:
- rhs: bfloat16 [4096, 1024], P(('space', 'sub')), may hold values from -6 to 6
- blocks: bfloat16 [4096, 7, 4096], P(('space', 'sub')), may hold values from -0.125 to 0.125
- columns: int32 [4096, 7], P(('space', 'sub')), may hold values from 0 to 639, as said below
- ghost_lists: int32 [32, 128], P(('space', 'sub')), may hold values from 0 to 127, as said below
Outputs:
- solution: float32 [4096, 1024], P(('space', 'sub'))
- residual: float32 [4096, 1024], P(('space', 'sub'))
Inputs may be any that keep to these rules, and one draw needn't show every extreme that they name: `columns`: for block row r (local) of device (p, q): entry 0 is q * 128 + r; entries 1 and 2 are q2 * 128 + ghost_lists[p * 4 + q2, k] for some q2 < 4 and k < 64; entries 3 and 4 lie in the part received from the previous subdomain, entries 5 and 6 in that from the next. `ghost_lists`: each row is a permutation of 0 .. 127.
All inputs are finite; a program needn't handle non-finite values.
Results may differ from a plain program's by a relative error of at most 0.0055.
Values may be sent and summed in bfloat16 or wider, within the bound.
A program may use at most 128 MiB of HBM per device.

v0:
```python
import jax
import jax.numpy as jnp
from jax import lax
from jax.sharding import PartitionSpec as P

BS = 64
NRHS = 16
NNZ = 7
S = 4


def shifted(value, axis, steps):
    count = lax.axis_size(axis)
    initial, last = (max(0, -steps), min(count, count - steps))
    return lax.ppermute(value, axis, [(source, source + steps) for source in range(initial, last)])


def finish(rhs, stack, gram):
    rows = stack.shape[0]
    paired = gram[1:] + gram[:-1]
    hmat = (paired[:, :, 1:] + paired[:, :, :-1]).reshape(S * NRHS, S * NRHS)
    cvec = paired[:, :, 0].reshape(S * NRHS, NRHS)
    lower = jnp.linalg.cholesky(hmat)
    coef = jax.scipy.linalg.cho_solve((lower, True), cvec).reshape(S, NRHS, NRHS)
    kfull = stack.astype(jnp.float32)
    highest = lax.Precision.HIGHEST
    sol = jnp.einsum("rjia,jac->ric", kfull[:, :S], coef, precision=highest)
    wmat = kfull[:, 1:] + kfull[:, :S]
    image = jnp.einsum("rjia,jac->ric", wmat, coef, precision=highest)
    res = rhs.astype(jnp.float32).reshape(rows, BS, NRHS) - image
    return (sol.reshape(rows, BS * NRHS), res.reshape(rows, BS * NRHS))


def on_device(rhs, blocks, columns, ghost_lists):
    rows = rhs.shape[0]
    ghost = ghost_lists.shape[1] // 2
    send_up = ghost_lists[0, :ghost]
    send_down = ghost_lists[0, ghost:]
    mats = blocks.reshape(rows, NNZ, BS, BS)
    basis = [rhs]
    for j in range(S):
        current = basis[-1]
        boundary = current[send_up]
        lower = shifted(boundary, "space", 1)
        upper = shifted(current[send_down], "space", -1)
        whole = lax.all_gather(current, "sub", axis=0, tiled=True)
        extended = jnp.concatenate([whole, lower, upper], axis=0)
        picked = extended[columns].reshape(rows, NNZ, BS, NRHS)
        nxt = jnp.einsum("rbij,rbjk->rik", mats, picked, preferred_element_type=jnp.float32)
        basis.append(nxt.astype(jnp.bfloat16).reshape(rows, BS * NRHS))
    stack = jnp.stack(basis, axis=1).reshape(rows, S + 1, BS, NRHS)
    partial_value = jnp.einsum("rjia,rkic->jakc", stack, stack, preferred_element_type=jnp.float32)
    gram = lax.psum(partial_value, ("space", "sub"))
    return finish(rhs, stack, gram)


def solution(mesh):
    in_specs = (
        P(("space", "sub"), None),
        P(("space", "sub"), None, None),
        P(("space", "sub"), None),
        P(("space", "sub"), None),
    )
    out_specs = (P(("space", "sub"), None), P(("space", "sub"), None))
    return jax.shard_map(
        on_device, mesh=mesh, in_specs=in_specs, out_specs=out_specs, check_vma=False
    )
```

profile of v0, /device:TPU:0, one launch (start us, length us, event | category | flops | bytes accessed | tf_op | source)
XLA Modules:
  0.0 319.2 jit_solution(4314674499148985406)
XLA Ops:
  7.2 0.7 all-gather.5.cloned.1.call-update
  8.0 0.8 fusion.27
  8.8 1.8 gather_fusion
  10.6 4.9 %collective-permute-start = (bf16[64,1024]{1,0:T(8,128)(2,1)S(1)}, bf16[64,1024]{1,0:T(8,128)(2,1)S(1)}, u32[]{:S(2)}, u32[]{:S(2)}) collective-permute-start(bf16[64,1024]{1,0:T(8,128)(2,1)S(1)} %gather_fusion), channel_id=1, source_target_pairs={{0,4},{4,8},{8,12},{12,16},{16,20},{20,24},{24,28},{1,5},{5,9},{9,... | collective-permute-start | bytes 393224 | tf_op jit(solution)/shard_map/ppermute | solution.py:15
  15.5 1.8 gather_fusion.1
  17.2 1.3 collective-permute-start.1
  19.1 10.9 %copy.27 = bf16[128,7,4096]{0,2,1:T(8,128)(2,1)} copy(bf16[128,7,4096]{2,0,1:T(8,128)(2,1)} %param.5) | data formatting | bytes 14680064 | tf_op args[1]
  30.0 21.2 %copy.29 = bf16[128,7,64,64]{3,2,1,0:T(8,128)(2,1)} copy(bf16[128,7,64,64]{0,3,2,1:T(8,128)(2,1)} %bitcast.114) | data formatting | bytes 14680064 | tf_op jit(solution)/shard_map/reshape | solution.py:39
  51.7 1.0 constant_dynamic-update-slice_fusion.3
  52.8 1.3 pad_maximum_fusion
  54.1 3.6 %gather_fusion.2 = bf16[896,1024]{1,0:T(8,128)(2,1)S(1)} fusion(bf16[640,1024]{1,0:T(8,128)(2,1)S(1)} %pad_maximum_fusion, s32[1024]{0:T(1024)S(1)} %pad_clamp_fusion), kind=kCustom, calls=%fused_computation.2 | custom fusion | bytes 3673600 | tf_op jit(solution)/shard_map/gather | solution.py:48
  57.7 13.8 %reshape.125 = bf16[128,7,64,16]{3,2,1,0:T(8,128)(2,1)} reshape(bf16[896,1024]{1,0:T(8,128)(2,1)S(1)} %gather_fusion.2) | data formatting | bytes 3670016 | tf_op jit(solution)/shard_map/reshape | solution.py:48
  71.5 12.5 %constant_dynamic-update-slice_fusion.2 = (bf16[128,5,64,16]{2,3,0,1:T(8,128)(2,1)}, bf16[128,16,64]{2,1,0:T(8,128)(2,1)S(1)}) fusion(bf16[128,5,64,16]{2,3,0,1:T(8,128)(2,1)} %constant_dynamic-update-slice_fusion.3, bf16[128,7,64,16]{3,2,1,0:T(8,128)(2,1)} %reshape.125, bf16[128,7,64,64]{3,2,1,0:T(8,128)(2,1)} %copy.29), kind=kOutput, calls=%fused_computation.57 | convolution fusion | flops 117571584 | bytes 30146560 | tf_op jit(solution)/shard_map/rbij,rbjk->rik/dot_general | solution.py:49
  84.1 0.6 copy.30
  84.7 0.9 copy.31
  85.6 1.8 gather_fusion.3
  87.4 1.8 gather_fusion.4
  89.2 4.4 %collective-permute-start.2 = (bf16[64,1024]{1,0:T(8,128)(2,1)S(1)}, bf16[64,1024]{1,0:T(8,128)(2,1)S(1)}, u32[]{:S(2)}, u32[]{:S(2)}) collective-permute-start(bf16[64,1024]{1,0:T(8,128)(2,1)S(1)} %gather_fusion.3), channel_id=1, source_target_pairs={{0,4},{4,8},{8,12},{12,16},{16,20},{20,24},{24,28},{1,5},{5,9},{9,... | collective-permute-start | bytes 393224 | tf_op jit(solution)/shard_map/ppermute | solution.py:15
  93.6 1.5 collective-permute-start.3
  95.1 1.0 collective-permute-done.2
  96.1 4.8 %collective-permute-done.3 = bf16[64,1024]{1,0:T(8,128)(2,1)S(1)} collective-permute-done((bf16[64,1024]{1,0:T(8,128)(2,1)S(1)}, bf16[64,1024]{1,0:T(8,128)(2,1)S(1)}, u32[]{:S(2)}, u32[]{:S(2)}) %collective-permute-start.3) | collective-permute-done | bytes 131104 | tf_op jit(solution)/shard_map/ppermute | solution.py:15
  100.8 3.8 %all-gather.7.cloned.1.call-done = bf16[512,1024]{1,0:T(8,128)(2,1)} async-done(((bf16[128,1024]{1,0:T(8,128)(2,1)}), bf16[512,1024]{1,0:T(8,128)(2,1)}) %all-gather.7.cloned.1.call-update) | async-done | bytes 1048592 | tf_op jit(solution)/shard_map/all_gather | solution.py:46
  104.6 1.3 pad_maximum_fusion.1
  106.0 3.6 %gather_fusion.5 = bf16[896,1024]{1,0:T(8,128)(2,1)S(1)} fusion(bf16[640,1024]{1,0:T(8,128)(2,1)S(1)} %pad_maximum_fusion.1, s32[1024]{0:T(1024)S(1)} %pad_clamp_fusion), kind=kCustom, calls=%fused_computation.5 | custom fusion | bytes 3673600 | tf_op jit(solution)/shard_map/gather | solution.py:48
  109.6 13.8 %reshape.128 = bf16[128,7,64,16]{3,2,1,0:T(8,128)(2,1)} reshape(bf16[896,1024]{1,0:T(8,128)(2,1)S(1)} %gather_fusion.5) | data formatting | bytes 3670016 | tf_op jit(solution)/shard_map/reshape | solution.py:48
  123.4 12.5 %constant_dynamic-update-slice_fusion.1 = (bf16[128,5,64,16]{2,3,0,1:T(8,128)(2,1)}, bf16[128,16,64]{2,1,0:T(8,128)(2,1)S(1)}) fusion(bf16[128,5,64,16]{2,3,0,1:T(8,128)(2,1)} %get-tuple-element.8, bf16[128,7,64,16]{3,2,1,0:T(8,128)(2,1)} %reshape.128, bf16[128,7,64,64]{3,2,1,0:T(8,128)(2,1)} %copy.29), kind=kOutput, calls=%fused_computation.56 | convolution fusion | flops 117571584 | bytes 30146560 | tf_op jit(solution)/shard_map/rbij,rbjk->rik/dot_general | solution.py:49
  135.9 0.6 copy.36
  136.5 0.9 copy.37
  137.5 1.8 gather_fusion.6
  139.2 1.8 gather_fusion.7
  141.0 3.4 %collective-permute-start.4 = (bf16[64,1024]{1,0:T(8,128)(2,1)S(1)}, bf16[64,1024]{1,0:T(8,128)(2,1)S(1)}, u32[]{:S(2)}, u32[]{:S(2)}) collective-permute-start(bf16[64,1024]{1,0:T(8,128)(2,1)S(1)} %gather_fusion.6), channel_id=1, source_target_pairs={{0,4},{4,8},{8,12},{12,16},{16,20},{20,24},{24,28},{1,5},{5,9},{9,... | collective-permute-start | bytes 393224 | tf_op jit(solution)/shard_map/ppermute | solution.py:15
  144.4 1.3 collective-permute-start.5
  145.7 1.8 collective-permute-done.4
  147.6 4.1 %collective-permute-done.5 = bf16[64,1024]{1,0:T(8,128)(2,1)S(1)} collective-permute-done((bf16[64,1024]{1,0:T(8,128)(2,1)S(1)}, bf16[64,1024]{1,0:T(8,128)(2,1)S(1)}, u32[]{:S(2)}, u32[]{:S(2)}) %collective-permute-start.5) | collective-permute-done | bytes 131104 | tf_op jit(solution)/shard_map/ppermute | solution.py:15
  151.7 2.6 all-gather.9.cloned.1.call-done
  154.3 1.3 pad_maximum_fusion.2
  155.6 3.6 %gather_fusion.8 = bf16[896,1024]{1,0:T(8,128)(2,1)S(1)} fusion(bf16[640,1024]{1,0:T(8,128)(2,1)S(1)} %pad_maximum_fusion.2, s32[1024]{0:T(1024)S(1)} %pad_clamp_fusion), kind=kCustom, calls=%fused_computation.8 | custom fusion | bytes 3673600 | tf_op jit(solution)/shard_map/gather | solution.py:48
  159.3 13.8 %reshape.130 = bf16[128,7,64,16]{3,2,1,0:T(8,128)(2,1)} reshape(bf16[896,1024]{1,0:T(8,128)(2,1)S(1)} %gather_fusion.8) | data formatting | bytes 3670016 | tf_op jit(solution)/shard_map/reshape | solution.py:48
  173.1 12.5 %constant_dynamic-update-slice_fusion = (bf16[128,5,64,16]{2,3,0,1:T(8,128)(2,1)}, bf16[128,16,64]{2,1,0:T(8,128)(2,1)S(1)}) fusion(bf16[128,5,64,16]{2,3,0,1:T(8,128)(2,1)} %get-tuple-element.10, bf16[128,7,64,16]{3,2,1,0:T(8,128)(2,1)} %reshape.130, bf16[128,7,64,64]{3,2,1,0:T(8,128)(2,1)} %copy.29), kind=kOutput, calls=%fused_computation.55 | convolution fusion | flops 117571584 | bytes 30146560 | tf_op jit(solution)/shard_map/rbij,rbjk->rik/dot_general | solution.py:49
  186.2 0.9 copy.44
  187.1 1.8 gather_fusion.9
  188.9 1.8 gather_fusion.10
  190.6 3.4 %collective-permute-start.6 = (bf16[64,1024]{1,0:T(8,128)(2,1)S(1)}, bf16[64,1024]{1,0:T(8,128)(2,1)S(1)}, u32[]{:S(2)}, u32[]{:S(2)}) collective-permute-start(bf16[64,1024]{1,0:T(8,128)(2,1)S(1)} %gather_fusion.9), channel_id=1, source_target_pairs={{0,4},{4,8},{8,12},{12,16},{16,20},{20,24},{24,28},{1,5},{5,9},{9,... | collective-permute-start | bytes 393224 | tf_op jit(solution)/shard_map/ppermute | solution.py:15
  194.0 1.5 collective-permute-start.7
  195.6 0.9 copy.56
  196.5 0.7 collective-permute-done.6
  197.2 4.1 %collective-permute-done.7 = bf16[64,1024]{1,0:T(8,128)(2,1)S(1)} collective-permute-done((bf16[64,1024]{1,0:T(8,128)(2,1)S(1)}, bf16[64,1024]{1,0:T(8,128)(2,1)S(1)}, u32[]{:S(2)}, u32[]{:S(2)}) %collective-permute-start.7) | collective-permute-done | bytes 131104 | tf_op jit(solution)/shard_map/ppermute | solution.py:15
  201.3 2.7 all-gather.11.cloned.1.call-done
  204.0 1.3 pad_maximum_fusion.3
  205.3 3.6 %gather_fusion.11 = bf16[896,1024]{1,0:T(8,128)(2,1)S(1)} fusion(bf16[640,1024]{1,0:T(8,128)(2,1)S(1)} %pad_maximum_fusion.3, s32[1024]{0:T(1024)S(1)} %pad_clamp_fusion), kind=kCustom, calls=%fused_computation.11 | custom fusion | bytes 3673600 | tf_op jit(solution)/shard_map/gather | solution.py:48
  208.9 13.8 %reshape.132 = bf16[128,7,64,16]{3,2,1,0:T(8,128)(2,1)} reshape(bf16[896,1024]{1,0:T(8,128)(2,1)S(1)} %gather_fusion.11) | data formatting | bytes 3670016 | tf_op jit(solution)/shard_map/reshape | solution.py:48
  222.7 12.5 %fusion.18 = bf16[128,5,64,16]{2,3,0,1:T(8,128)(2,1)} fusion(bf16[128,5,64,16]{2,3,0,1:T(8,128)(2,1)} %get-tuple-element.12, bf16[128,7,64,16]{3,2,1,0:T(8,128)(2,1)} %reshape.132, bf16[128,7,64,64]{3,2,1,0:T(8,128)(2,1)} %copy.29), kind=kOutput, calls=%fused_computation.39 | convolution fusion | flops 117571584 | bytes 29884416 | tf_op jit(solution)/shard_map/rbij,rbjk->rik/dot_general | solution.py:49
  235.3 4.7 %convert_element_type.36 = f32[128,5,64,16]{2,3,0,1:T(8,128)} convert(bf16[128,5,64,16]{2,3,0,1:T(8,128)(2,1)} %fusion.18) | non-fusion elementwise | flops 655360 | bytes 3932160 | tf_op jit(solution)/shard_map/convert_element_type | solution.py:25
  240.0 3.8 %fusion.19 = f32[5,16,5,16]{3,1,2,0:T(8,128)S(1)} fusion(bf16[128,5,64,16]{2,3,0,1:T(8,128)(2,1)S(1)} %copy-done.1), kind=kOutput, calls=%fused_computation.40 | convolution fusion | flops 104857600 | bytes 1336320 | tf_op jit(solution)/shard_map/rjia,rkic->jakc/dot_general | solution.py:52
  243.8 43.3 %psum.7 = f32[5,16,5,16]{3,1,2,0:T(8,128)S(1)} all-reduce(f32[5,16,5,16]{3,1,2,0:T(8,128)S(1)} %fusion.19), channel_id=1, replica_groups=mesh['space'=8,'sub'=4] {'space','sub'}, use_global_device_ids=true, to_apply=%region_0.0 | all-reduce | flops 6400 | bytes 51200 | tf_op jit(solution)/shard_map/psum | solution.py:53
  287.5 5.8 %cholesky.16 = f32[64,64]{1,0:T(8,128)S(1)} custom-call(f32[64,64]{1,0:T(8,128)S(1)} %fusion.26), custom_call_target="Cholesky" | custom-call | tf_op jit(solution)/shard_map/jit(cholesky)/cholesky | solution.py:23
  293.4 0.7 compare_reduce_fusion
  294.6 4.9 %custom-call.10 = f32[1,64,64]{1,2,0:T(8,128)S(1)} custom-call(f32[1,64,64]{2,1,0:T(8,128)S(1)} %fusion.24), custom_call_target="InvertDiagBlocksLowerTriangular" | custom-call | tf_op jit(solution)/shard_map/jit(_cho_solve)/triangular_solve | solution.py:24
  300.1 4.8 %fusion = f32[128,64,16,1]{1,2,0,3:T(8,128)S(1)} fusion(f32[4,16,16,1]{1,2,3,0:T(8,128)S(1)} %convolution_bitcast_fusion.4, f32[128,5,64,16]{2,3,0,1:T(8,128)} %convert_element_type.36), kind=kOutput, calls=%fused_computation.13 | convolution fusion | flops 101187584 | bytes 8916992 | tf_op jit(solution)/shard_map/rjia,jac->ric/dot_general | solution.py:29
  305.5 1.2 bitcast_subtract_fusion
  306.7 1.0 copy.60
  307.7 2.2 fusion.5
  309.9 1.7 copy.75
  311.6 1.0 copy.59
  (53 shorter events, 4.0 us)
Async XLA Ops:
  7.2 11.7 %copy-start = (bf16[128,1024]{1,0:T(8,128)(2,1)S(1)}, bf16[128,1024]{1,0:T(8,128)(2,1)}, u32[]{:S(2)}) copy-start(bf16[128,1024]{1,0:T(8,128)(2,1)} %param.4) | copy-start | bytes 786436
  7.2 11.4 %copy-start.10 = (s32[128,7]{0,1:T(8,128)S(1)}, s32[128,7]{0,1:T(8,128)}, u32[]{:S(2)}) copy-start(s32[128,7]{0,1:T(8,128)} %param.6) | copy-start | bytes 10756
  7.2 45.6 %all-gather.5.cloned.1.call-start = ((), (), s32[]{:S(2)}) async-start(), calls=%async_computation | async-start | bytes 1310720 | tf_op jit(solution)/shard_map/all_gather | solution.py:46
  7.9 96.7 %all-gather.7.cloned.1.call-start = ((), (), s32[]{:S(2)}) async-start(), calls=%async_computation.1 | async-start | bytes 1310720 | tf_op jit(solution)/shard_map/all_gather | solution.py:46
  10.6 42.1 %collective-permute-start = (bf16[64,1024]{1,0:T(8,128)(2,1)S(1)}, bf16[64,1024]{1,0:T(8,128)(2,1)S(1)}, u32[]{:S(2)}, u32[]{:S(2)}) collective-permute-start(bf16[64,1024]{1,0:T(8,128)(2,1)S(1)} %gather_fusion), channel_id=1, source_target_pairs={{0,4},{4,8},{8,12},{12,16},{16,20},{20,24},{24,28},{1,5},{5,9},{9,... | collective-permute-start | bytes 393224 | tf_op jit(solution)/shard_map/ppermute | solution.py:15
  17.2 35.5 %collective-permute-start.1 = (bf16[64,1024]{1,0:T(8,128)(2,1)S(1)}, bf16[64,1024]{1,0:T(8,128)(2,1)S(1)}, u32[]{:S(2)}, u32[]{:S(2)}) collective-permute-start(bf16[64,1024]{1,0:T(8,128)(2,1)S(1)} %gather_fusion.1), channel_id=1, source_target_pairs={{4,0},{8,4},{12,8},{16,12},{20,16},{24,20},{28,24},{5,1},{9,5},{13... | collective-permute-start | bytes 393224 | tf_op jit(solution)/shard_map/ppermute | solution.py:15
  51.7 1.0 copy-start.8
  84.1 16.8 %copy-start.2 = (bf16[128,16,64]{2,1,0:T(8,128)(2,1)}, bf16[128,16,64]{2,1,0:T(8,128)(2,1)S(1)}, u32[]{:S(2)}) copy-start(bf16[128,16,64]{2,1,0:T(8,128)(2,1)S(1)} %get-tuple-element.9) | copy-start | bytes 786436
  85.5 68.8 %all-gather.9.cloned.1.call-start = ((), (), s32[]{:S(2)}) async-start(), calls=%async_computation.2 | async-start | bytes 1310720 | tf_op jit(solution)/shard_map/all_gather | solution.py:46
  89.2 6.9 %collective-permute-start.2 = (bf16[64,1024]{1,0:T(8,128)(2,1)S(1)}, bf16[64,1024]{1,0:T(8,128)(2,1)S(1)}, u32[]{:S(2)}, u32[]{:S(2)}) collective-permute-start(bf16[64,1024]{1,0:T(8,128)(2,1)S(1)} %gather_fusion.3), channel_id=1, source_target_pairs={{0,4},{4,8},{8,12},{12,16},{16,20},{20,24},{24,28},{1,5},{5,9},{9,... | collective-permute-start | bytes 393224 | tf_op jit(solution)/shard_map/ppermute | solution.py:15
  93.6 7.3 %collective-permute-start.3 = (bf16[64,1024]{1,0:T(8,128)(2,1)S(1)}, bf16[64,1024]{1,0:T(8,128)(2,1)S(1)}, u32[]{:S(2)}, u32[]{:S(2)}) collective-permute-start(bf16[64,1024]{1,0:T(8,128)(2,1)S(1)} %gather_fusion.4), channel_id=1, source_target_pairs={{4,0},{8,4},{12,8},{16,12},{20,16},{24,20},{28,24},{5,1},{9,5},{13... | collective-permute-start | bytes 393224 | tf_op jit(solution)/shard_map/ppermute | solution.py:15
  135.9 15.7 %copy-start.4 = (bf16[128,16,64]{2,1,0:T(8,128)(2,1)}, bf16[128,16,64]{2,1,0:T(8,128)(2,1)S(1)}, u32[]{:S(2)}) copy-start(bf16[128,16,64]{2,1,0:T(8,128)(2,1)S(1)} %get-tuple-element.11) | copy-start | bytes 786436
  137.4 66.5 %all-gather.11.cloned.1.call-start = ((), (), s32[]{:S(2)}) async-start(), calls=%async_computation.3 | async-start | bytes 1310720 | tf_op jit(solution)/shard_map/all_gather | solution.py:46
  141.0 6.5 %collective-permute-start.4 = (bf16[64,1024]{1,0:T(8,128)(2,1)S(1)}, bf16[64,1024]{1,0:T(8,128)(2,1)S(1)}, u32[]{:S(2)}, u32[]{:S(2)}) collective-permute-start(bf16[64,1024]{1,0:T(8,128)(2,1)S(1)} %gather_fusion.6), channel_id=1, source_target_pairs={{0,4},{4,8},{8,12},{12,16},{16,20},{20,24},{24,28},{1,5},{5,9},{9,... | collective-permute-start | bytes 393224 | tf_op jit(solution)/shard_map/ppermute | solution.py:15
  144.4 7.2 %collective-permute-start.5 = (bf16[64,1024]{1,0:T(8,128)(2,1)S(1)}, bf16[64,1024]{1,0:T(8,128)(2,1)S(1)}, u32[]{:S(2)}, u32[]{:S(2)}) collective-permute-start(bf16[64,1024]{1,0:T(8,128)(2,1)S(1)} %gather_fusion.7), channel_id=1, source_target_pairs={{4,0},{8,4},{12,8},{16,12},{20,16},{24,20},{28,24},{5,1},{9,5},{13... | collective-permute-start | bytes 393224 | tf_op jit(solution)/shard_map/ppermute | solution.py:15
  185.6 15.7 %copy-start.6 = (bf16[128,16,64]{2,1,0:T(8,128)(2,1)}, bf16[128,16,64]{2,1,0:T(8,128)(2,1)S(1)}, u32[]{:S(2)}) copy-start(bf16[128,16,64]{2,1,0:T(8,128)(2,1)S(1)} %get-tuple-element.13) | copy-start | bytes 786436
  190.6 6.5 %collective-permute-start.6 = (bf16[64,1024]{1,0:T(8,128)(2,1)S(1)}, bf16[64,1024]{1,0:T(8,128)(2,1)S(1)}, u32[]{:S(2)}, u32[]{:S(2)}) collective-permute-start(bf16[64,1024]{1,0:T(8,128)(2,1)S(1)} %gather_fusion.9), channel_id=1, source_target_pairs={{0,4},{4,8},{8,12},{12,16},{16,20},{20,24},{24,28},{1,5},{5,9},{9,... | collective-permute-start | bytes 393224 | tf_op jit(solution)/shard_map/ppermute | solution.py:15
  194.0 7.2 %collective-permute-start.7 = (bf16[64,1024]{1,0:T(8,128)(2,1)S(1)}, bf16[64,1024]{1,0:T(8,128)(2,1)S(1)}, u32[]{:S(2)}, u32[]{:S(2)}) collective-permute-start(bf16[64,1024]{1,0:T(8,128)(2,1)S(1)} %gather_fusion.10), channel_id=1, source_target_pairs={{4,0},{8,4},{12,8},{16,12},{20,16},{24,20},{28,24},{5,1},{9,5},{13... | collective-permute-start | bytes 393224 | tf_op jit(solution)/shard_map/ppermute | solution.py:15
  235.3 4.7 %copy-start.1 = (bf16[128,5,64,16]{2,3,0,1:T(8,128)(2,1)S(1)}, bf16[128,5,64,16]{2,3,0,1:T(8,128)(2,1)}, u32[]{:S(2)}) copy-start(bf16[128,5,64,16]{2,3,0,1:T(8,128)(2,1)} %fusion.18) | copy-start | bytes 3932164
  304.9 2.8 copy-start.3
  304.9 2.8 copy-start.5
  304.9 2.8 copy-start.7
  305.5 2.2 copy-start.9
Sparse Core Ops, SparseCore 0:
  9.6 19.4 all-gather.4
  85.6 18.9 all-gather.6
  137.5 16.7 all-gather.8
  187.2 16.7 all-gather.10
where the time goes:
time: 321 us; the launch traced here: 319 us
  local copies, waits for them, and re-layouts  128 us (40%)
  matrix products  61.5 us (19%)
  blocking collectives  43.3 us (13%)
  waiting for transfers between devices  26.3 us (8%)
  other arithmetic  24.1 us (8%)
  starting transfers between devices  21.8 us (7%)
  between operations  14.2 us (4%)
    reshape x4, local copies, waits for them, and re-layouts, on_device(): picked = extended[columns].reshape(rows, NNZ, BS, NRHS)  55.2 us
    dot_general x4, matrix products, on_device(): jnp.einsum('rbij,rbjk->rik', mats, picked, preferred_element_type=jnp.flo...  50.1 us
    psum x1, blocking collectives, on_device(): gram = lax.psum(partial_value, ('space', 'sub'))  43.3 us
    ppermute x8, starting transfers between devices, shifted(): lax.ppermute(value, axis, [(source, source + steps) for source in range(i...  21.6 us
    reshape x1, local copies, waits for them, and re-layouts, on_device(): mats = blocks.reshape(rows, NNZ, BS, BS)  21.2 us
    ppermute x8, waiting for transfers between devices, shifted(): lax.ppermute(value, axis, [(source, source + steps) for source in range(i...  16.5 us
    gather x4, local copies, waits for them, and re-layouts, on_device(): picked = extended[columns].reshape(rows, NNZ, BS, NRHS)  14.4 us
    unnamed x27, local copies, waits for them, and re-layouts  14.1 us
  transfers between devices with their start and end apart: 12, of which 9 were waited for; matrix products, arithmetic and copies ran while one was open for 16% of the time, Pallas kernels for 0%

commit v1 on v0

v1 whole, which is shorter than its diff:
```python
import functools

import jax
import jax.numpy as jnp
from jax import lax
from jax.experimental import pallas as pl
from jax.experimental.pallas import tpu as pltpu
from jax.sharding import PartitionSpec as P

BS = 64
NRHS = 16
NNZ = 7
S = 4
MESH = pl.DeviceIdType.MESH
NT = (((1,), (1,)), ((), ()))
CHUNKS = 4


def log2(n):
    return n.bit_length() - 1


def powers_kernel(
    n_space, n_sub, rows, ghost,
    index_ref, list_ref, first_ref, blocks_ref,
    gram_ref, basis_ref,
    raw, mats, turn, ext, fresh, up, down, near, low, high, gsend, grecv,
    load_sem, send_sem, recv_sem, gsend_sem, grecv_sem,
):
    p = lax.axis_index("space")
    q = lax.axis_index("sub")
    half = ghost // 2
    pairs = rows // 2
    rounds_sub, rounds_space = log2(n_sub), log2(n_space)
    has_low = p > 0
    has_high = p < n_space - 1

    per = rows // CHUNKS
    loads = [
        pltpu.make_async_copy(
            blocks_ref.at[pl.ds(n * per, per)], raw.at[pl.ds(n * per, per)], load_sem.at[n]
        )
        for n in range(CHUNKS)
    ]
    for load in loads:
        load.start()

    def flip(index, step):
        return index + step * (1 - 2 * ((index // step) % 2))

    barrier = pltpu.get_barrier_semaphore()
    for d in range(1, n_sub):
        pl.semaphore_signal(barrier, inc=1, device_id=(p, (q + d) % n_sub), device_id_type=MESH)
    for r in range(1, rounds_space):
        pl.semaphore_signal(barrier, inc=1, device_id=(flip(p, 1 << r), q), device_id_type=MESH)

    @pl.when(has_low)
    def _():
        pl.semaphore_signal(barrier, inc=1, device_id=(p - 1, q), device_id_type=MESH)

    @pl.when(has_high)
    def _():
        pl.semaphore_signal(barrier, inc=1, device_id=(p + 1, q), device_id_type=MESH)

    left16 = lax.broadcasted_iota(jnp.int32, (NRHS, 128), 1) < BS
    left32 = lax.broadcasted_iota(jnp.int32, (32, 128), 1) < BS
    src = lax.broadcasted_iota(jnp.int32, (128, 256), 0)
    dst = lax.broadcasted_iota(jnp.int32, (128, 256), 1)
    src_c = 2 * (src % 32) + (src // 32) % 2
    order = jnp.where((src // BS == dst // 128) & (src_c == dst % BS), 1.0, 0.0).astype(jnp.bfloat16)
    double = jnp.where((src // BS == dst // 128) & (src % BS == dst % BS), 1.0, 0.0).astype(jnp.bfloat16)

    def own_start(m, carry):
        even, odd = first_ref[2 * m], first_ref[2 * m + 1]
        ext[2 * m] = even
        ext[2 * m + 1] = odd
        basis_ref[0, m] = jnp.where(left16, even, odd)
        return carry

    lax.fori_loop(0, pairs, own_start, 0)

    def zero(m, carry):
        ext[rows + n_sub * ghost + m] = jnp.zeros((NRHS, 128), jnp.bfloat16)
        return carry

    lax.fori_loop(0, 2 * ghost, zero, 0)

    def copies(j):
        near_copies = [
            pltpu.make_async_remote_copy(
                src_ref=up.at[j], dst_ref=near.at[j, d - 1],
                send_sem=send_sem.at[j, d - 1], recv_sem=recv_sem.at[j, d - 1],
                device_id=(p, (q + d) % n_sub), device_id_type=MESH,
            )
            for d in range(1, n_sub)
        ]
        up_copy = pltpu.make_async_remote_copy(
            src_ref=up.at[j], dst_ref=low.at[j],
            send_sem=send_sem.at[j, n_sub - 1], recv_sem=recv_sem.at[j, n_sub - 1],
            device_id=((p + 1) % n_space, q), device_id_type=MESH,
        )
        down_copy = pltpu.make_async_remote_copy(
            src_ref=down.at[j], dst_ref=high.at[j],
            send_sem=send_sem.at[j, n_sub], recv_sem=recv_sem.at[j, n_sub],
            device_id=((p + n_space - 1) % n_space, q), device_id_type=MESH,
        )
        return near_copies, up_copy, down_copy

    def send(j):
        near_copies, up_copy, down_copy = copies(j)

        def pack_up(m, carry):
            up[j, m] = jnp.where(left16, ext[list_ref[2 * m]], ext[list_ref[2 * m + 1]])
            return carry

        def pack_down(m, carry):
            down[j, m] = jnp.where(
                left16, ext[list_ref[ghost + 2 * m]], ext[list_ref[ghost + 2 * m + 1]]
            )
            return carry

        lax.fori_loop(0, half, pack_up, 0, unroll=4)
        if j == 0:
            greeted = (n_sub - 1) + (rounds_space - 1)
            pl.semaphore_wait(barrier, greeted + jnp.where(has_low, 1, 0) + jnp.where(has_high, 1, 0))
        pl.when(has_high)(up_copy.start)
        for copy in near_copies:
            copy.start()
        lax.fori_loop(0, half, pack_down, 0, unroll=4)
        pl.when(has_low)(down_copy.start)

    def spread(buffer, lead, base):
        def body(m, carry):
            part = buffer[lead + (pl.ds(4 * m, 4),)].reshape(4 * NRHS, 128)
            wide = jnp.dot(part, double, preferred_element_type=jnp.float32).astype(jnp.bfloat16)
            for h in range(4):
                rows_h = wide[h * NRHS:(h + 1) * NRHS]
                ext[base + 8 * m + 2 * h] = rows_h[:, :128]
                ext[base + 8 * m + 2 * h + 1] = rows_h[:, 128:]
            return carry

        lax.fori_loop(0, half // 4, body, 0)

    def receive(j):
        near_copies, up_copy, down_copy = copies(j)
        for d, copy in enumerate(near_copies):
            copy.wait_recv()
            spread(near, (j, d), rows + d * ghost)

        @pl.when(has_low)
        def _():
            up_copy.wait_recv()
            spread(low, (j,), rows + n_sub * ghost)

        @pl.when(has_high)
        def _():
            down_copy.wait_recv()
            spread(high, (j,), rows + n_sub * ghost + ghost)

    def sent(j):
        near_copies, up_copy, down_copy = copies(j)
        for copy in near_copies:
            copy.wait_send()
        pl.when(has_high)(up_copy.wait_send)
        pl.when(has_low)(down_copy.wait_send)

    def relay(i, carry):
        for t in range(32):
            turn[t * 8:t * 8 + NNZ, :] = raw[i, :, t * 128:(t + 1) * 128].astype(jnp.float32)
        planes = [turn[pl.ds(b, 32, stride=8), :] for b in range(NNZ)]
        swapped = [pltpu.roll(plane, BS, 1) for plane in planes]
        zeros = jnp.zeros((32, 128), jnp.float32)
        planes.append(zeros)
        swapped.append(zeros)
        for m in range(4):
            a, b = 2 * m, 2 * m + 1
            mats[i, 0:32, m * 128:(m + 1) * 128] = jnp.where(left32, planes[a], swapped[b]).astype(jnp.bfloat16)
            mats[i, 32:64, m * 128:(m + 1) * 128] = jnp.where(left32, swapped[a], planes[b]).astype(jnp.bfloat16)
        return carry

    def product(j):
        def body(g, carry):
            lines = []
            for u in range(4):
                at = (4 * g + u) * NNZ
                tiles = [ext[index_ref[at + b]] for b in range(NNZ)]
                lines.append(jnp.concatenate(
                    [jnp.where(left16, tiles[2 * m], tiles[2 * m + 1]) for m in range(3)] + [tiles[6]], axis=1
                ))
            lhs = jnp.concatenate(lines, axis=0)
            rhs = mats[pl.ds(4 * g, 4)].reshape(4 * BS, 512)
            full = lax.dot_general(lhs, rhs, NT, preferred_element_type=jnp.float32)
            left = left16
            picked = [
                jnp.where(
                    left,
                    full[2 * h * NRHS:(2 * h + 1) * NRHS, h * 128:(h + 1) * 128],
                    full[(2 * h + 1) * NRHS:(2 * h + 2) * NRHS, h * 128:(h + 1) * 128],
                ).astype(jnp.bfloat16)
                for h in range(2)
            ]
            wide = jnp.dot(
                jnp.concatenate(picked, axis=0), order, preferred_element_type=jnp.float32
            ).astype(jnp.bfloat16)
            for h in range(2):
                even = wide[h * NRHS:(h + 1) * NRHS, :128]
                odd = wide[h * NRHS:(h + 1) * NRHS, 128:]
                fresh[4 * g + 2 * h] = even
                fresh[4 * g + 2 * h + 1] = odd
                basis_ref[j + 1, 2 * g + h] = jnp.where(left16, even, odd)
            return carry

        lax.fori_loop(0, rows // 4, body, 0)

        def take(m, carry):
            ext[m] = fresh[m]
            return carry

        if j < S - 1:
            lax.fori_loop(0, rows, take, 0, unroll=8)

    for j in range(S):
        send(j)
        if j == 0:
            for n in range(CHUNKS):
                loads[n].wait()
                lax.fori_loop(n * per, (n + 1) * per, relay, 0)
        receive(j)
        product(j)
        sent(j)

    width = (S + 1) * NRHS

    def gram_step(m, total):
        tile = jnp.concatenate(
            [basis_ref[:, 2 * m + h].reshape(width, 128) for h in range(2)], axis=1
        )
        return total + lax.dot_general(tile, tile, NT, preferred_element_type=jnp.float32)

    total = lax.fori_loop(0, pairs // 2, gram_step, jnp.zeros((width, width), jnp.float32))
    rounds = rounds_sub + rounds_space
    gsend[...] = jnp.zeros_like(gsend)
    gsend[0, :, :width] = total
    for r in range(rounds):
        if r < rounds_sub:
            partner = (p, flip(q, 1 << r))
        else:
            partner = (flip(p, 1 << (r - rounds_sub)), q)
        copy = pltpu.make_async_remote_copy(
            src_ref=gsend.at[r], dst_ref=grecv.at[r],
            send_sem=gsend_sem.at[r], recv_sem=grecv_sem.at[r],
            device_id=partner, device_id_type=MESH,
        )
        copy.start()
        copy.wait()
        if r < rounds - 1:
            gsend[r + 1] = gsend[r] + grecv[r]
        else:
            gram_ref[...] = gsend[r] + grecv[r]


def powers(n_space, n_sub, index, lists, first, blocks):
    rows = blocks.shape[0]
    ghost = lists.shape[0] // 2
    half = ghost // 2
    width = (S + 1) * NRHS
    rounds = log2(n_sub) + log2(n_space)
    bf, f32 = jnp.bfloat16, jnp.float32
    return pl.pallas_call(
        functools.partial(powers_kernel, n_space, n_sub, rows, ghost),
        out_shape=(
            jax.ShapeDtypeStruct((width, 128), f32),
            jax.ShapeDtypeStruct((S + 1, rows // 2, NRHS, 128), bf),
        ),
        in_specs=[
            pl.BlockSpec(memory_space=pltpu.SMEM),
            pl.BlockSpec(memory_space=pltpu.SMEM),
            pl.BlockSpec(memory_space=pltpu.VMEM),
            pl.BlockSpec(memory_space=pl.ANY),
        ],
        out_specs=[pl.BlockSpec(memory_space=pltpu.VMEM)] * 2,
        scratch_shapes=[
            pltpu.VMEM((rows, NNZ, BS * BS), bf),
            pltpu.VMEM((rows, BS, 512), bf),
            pltpu.VMEM((256, 128), f32),
            pltpu.VMEM((rows + n_sub * ghost + 2 * ghost, NRHS, 128), bf),
            pltpu.VMEM((rows, NRHS, 128), bf),
            pltpu.VMEM((S, half, NRHS, 128), bf),
            pltpu.VMEM((S, half, NRHS, 128), bf),
            pltpu.VMEM((S, n_sub - 1, half, NRHS, 128), bf),
            pltpu.VMEM((S, half, NRHS, 128), bf),
            pltpu.VMEM((S, half, NRHS, 128), bf),
            pltpu.VMEM((rounds, width, 128), f32),
            pltpu.VMEM((rounds, width, 128), f32),
            pltpu.SemaphoreType.DMA((CHUNKS,)),
            pltpu.SemaphoreType.DMA((S, n_sub + 1)),
            pltpu.SemaphoreType.DMA((S, n_sub + 1)),
            pltpu.SemaphoreType.DMA((rounds,)),
            pltpu.SemaphoreType.DMA((rounds,)),
        ],
        compiler_params=pltpu.CompilerParams(
            collective_id=0, has_side_effects=True, vmem_limit_bytes=56 * 1024 * 1024
        ),
    )(index, lists, first, blocks)


def finish(rhs, stack, gram):
    rows = stack.shape[0]
    paired = gram[1:] + gram[:-1]
    hmat = (paired[:, :, 1:] + paired[:, :, :-1]).reshape(S * NRHS, S * NRHS)
    cvec = paired[:, :, 0].reshape(S * NRHS, NRHS)
    lower = jnp.linalg.cholesky(hmat)
    coef = jax.scipy.linalg.cho_solve((lower, True), cvec).reshape(S, NRHS, NRHS)
    kfull = stack.astype(jnp.float32)
    highest = lax.Precision.HIGHEST
    sol = jnp.einsum("rjia,jac->ric", kfull[:, :S], coef, precision=highest)
    wmat = kfull[:, 1:] + kfull[:, :S]
    image = jnp.einsum("rjia,jac->ric", wmat, coef, precision=highest)
    res = rhs.astype(jnp.float32).reshape(rows, BS, NRHS) - image
    return (sol.reshape(rows, BS * NRHS), res.reshape(rows, BS * NRHS))


def on_device(rhs, blocks, columns, ghost_lists):
    n_space, n_sub = lax.axis_size("space"), lax.axis_size("sub")
    rows = rhs.shape[0]
    ghost = ghost_lists.shape[1] // 2
    q = lax.axis_index("sub")
    lists = ghost_lists[0]
    every = lax.all_gather(lists, "sub", axis=0)
    near = columns[:, 1:3]
    peer, row = near // rows, near % rows
    owner = jnp.arange(n_sub, dtype=jnp.int32)
    match = (peer[..., None, None] == owner[:, None]) & (row[..., None, None] == every[:, :ghost])
    place = jnp.sum(jnp.where(match, jnp.arange(ghost, dtype=jnp.int32), 0), axis=(2, 3))
    slot = (q - peer - 1) % n_sub
    near = jnp.where(peer == q, row, rows + slot * ghost + place)
    far = columns[:, 3:] - n_sub * rows + rows + n_sub * ghost
    local = jnp.arange(rows, dtype=jnp.int32)[:, None]
    index = jnp.concatenate([local, near, far], axis=1).reshape(-1)
    first = rhs.reshape(rows, BS, NRHS).transpose(0, 2, 1)
    first = jnp.concatenate([first, first], axis=2)
    gram, basis = powers(n_space, n_sub, index, lists, first, blocks)
    width = (S + 1) * NRHS
    gram = gram[:, :width].reshape(S + 1, NRHS, S + 1, NRHS)
    stack = basis.reshape(S + 1, rows // 2, NRHS, 2, BS).transpose(1, 3, 0, 4, 2)
    return finish(rhs, stack.reshape(rows, S + 1, BS, NRHS), gram)


def solution(mesh):
    in_specs = (
        P(("space", "sub"), None),
        P(("space", "sub"), None, None),
        P(("space", "sub"), None),
        P(("space", "sub"), None),
    )
    out_specs = (P(("space", "sub"), None), P(("space", "sub"), None))
    return jax.shard_map(
        on_device, mesh=mesh, in_specs=in_specs, out_specs=out_specs, check_vma=False
    )
```

time: 321 us -> 178 us (0.55)
  Pallas kernels: 0 us -> 119 us
  local copies, waits for them, and re-layouts: 128 us -> 31 us
  matrix products: 61.5 us -> 4.73 us
  blocking collectives: 43.3 us -> 6.15 us
  waiting for transfers between devices: 26.3 us -> 0 us
  starting transfers between devices: 21.8 us -> 0 us
  between operations: 14.2 us -> 0.77 us
  other arithmetic: 24.1 us -> 16.2 us
    pallas_call x0 -> x1, Pallas kernels: none -> 119 us  [powers(): pl.pallas_call(functools.partial(powers_kernel, n_space, n_sub, rows, gho...]
    reshape x9 -> x4, local copies, waits for them, and re-layouts: 80 us -> 9.08 us  [the longest x2 7.75 us: on_device(): basis.reshape(S + 1, rows // 2, NRHS, 2, BS).transpose(1, 3, 0, 4, 2)]
    dot_general x5 -> x0, matrix products: 53.9 us -> none  [the longest x4 50.1 us: on_device(): jnp.einsum('rbij,rbjk->rik', mats, picked, preferred_element_type=jnp.flo...]
    psum x1 -> x0, blocking collectives: 43.3 us -> none  [on_device(): gram = lax.psum(partial_value, ('space', 'sub'))]
    gather x12 -> x0, local copies, waits for them, and re-layouts: 28.7 us -> none  [the longest x4 14.4 us: on_device(): picked = extended[columns].reshape(rows, NNZ, BS, NRHS)]
    ppermute x8 -> x0, starting transfers between devices: 21.6 us -> none  [shifted(): lax.ppermute(value, axis, [(source, source + steps) for source in range(i...]
    ppermute x8 -> x0, waiting for transfers between devices: 16.5 us -> none  [shifted(): lax.ppermute(value, axis, [(source, source + steps) for source in range(i...]
    all_gather x4 -> x0, waiting for transfers between devices: 9.08 us -> none  [on_device(): whole = lax.all_gather(current, 'sub', axis=0, tiled=True)]
  transfers between devices with their start and end apart: 12 -> 0, of which waited for: 9 -> 0; matrix products, arithmetic and copies ran while one was open for 16% -> 0% of each run, Pallas kernels for 0% -> 0%
where the time goes in v1:
time: 178 us; the launch traced here: 177 us
  Pallas kernels  119 us (67%)
  local copies, waits for them, and re-layouts  31 us (17%)
  other arithmetic  16.2 us (9%)
  blocking collectives  6.15 us (3%)
  matrix products  4.73 us (3%)
    pallas_call x1, Pallas kernels, powers(): pl.pallas_call(functools.partial(powers_kernel, n_space, n_sub, rows, gho...  119 us
    unnamed x5, local copies, waits for them, and re-layouts  18.7 us
    reshape x2, local copies, waits for them, and re-layouts, on_device(): basis.reshape(S + 1, rows // 2, NRHS, 2, BS).transpose(1, 3, 0, 4, 2)  7.75 us
    another operation x3, other arithmetic, finish(): lower = jnp.linalg.cholesky(hmat)  6.52 us
    all_gather x1, blocking collectives, on_device(): every = lax.all_gather(lists, 'sub', axis=0)  6.15 us
    another operation x2, other arithmetic, finish(): jax.scipy.linalg.cho_solve((lower, True), cvec).reshape(S, NRHS, NRHS)  5.55 us

profile of v1, /device:TPU:0, one launch (start us, length us, event | category | flops | bytes accessed | tf_op | source)
XLA Modules:
  0.0 177.5 jit_solution(12303703769526519347)
XLA Ops:
  0.6 6.1 %all-gather = s32[4,1,128]{2,1,0:T(1,128)S(1)} all-gather(s32[1,1,128]{2,1,0:T(1,128)} %bitcast.58), channel_id=1, replica_groups=mesh['space'=8,'sub'=4] {'sub'}, dimensions={0}, use_global_device_ids=true | all-gather | bytes 2560 | tf_op jit(solution)/shard_map/all_gather | solution.py:329
  6.8 0.7 slice_add_fusion.6
  7.5 0.7 and_select_fusion.2
  8.2 0.1 select_reduce_fusion
  8.4 0.1 copy.62
  8.5 0.8 reshape.58.index_ref
  9.3 1.1 copy.63
  10.4 0.5 copy.64
  10.9 1.1 pad_maximum_fusion.first_ref
  12.0 10.4 %copy.65.blocks_ref = bf16[128,7,4096]{2,1,0:T(8,128)(2,1)} copy(bf16[128,7,4096]{2,0,1:T(8,128)(2,1)} %param.5) | data formatting | bytes 14680064 | tf_op args[1]
  22.4 118.6 %shard_map.59 = (f32[80,128]{1,0:T(8,128)}, bf16[5,64,16,128]{3,2,1,0:T(8,128)(2,1)}) custom-call(s32[896]{0:T(1024)} %reshape.58.index_ref, s32[128]{0:T(128)} %bitcast.59, bf16[128,16,128]{2,1,0:T(8,128)(2,1)} %pad_maximum_fusion.first_ref, bf16[128,7,4096]{2,1,0:T(8,128)(2,1)} %copy.65.blocks_ref), custom_call_target="tpu_custom_call" | custom-call | tf_op jit(solution)/shard_map/pallas_call | solution.py:269
  141.0 0.8 slice_add_fusion.5
  141.9 0.1 copy.68
  141.9 0.1 add.66
  142.1 0.1 reshape.62
  142.2 0.1 reshape_squeeze.3
  142.3 0.1 copy.69
  142.4 5.8 %cholesky.16 = f32[64,64]{1,0:T(8,128)S(1)} custom-call(f32[64,64]{1,0:T(8,128)S(1)} %fusion.5), custom_call_target="Cholesky" | custom-call | tf_op jit(solution)/shard_map/jit(cholesky)/cholesky | solution.py:312
  148.3 0.6 compare_reduce_fusion
  148.9 0.7 fusion.3
  149.6 4.9 %custom-call.10 = f32[1,64,64]{1,2,0:T(8,128)S(1)} custom-call(f32[1,64,64]{2,1,0:T(8,128)S(1)} %fusion.3), custom_call_target="InvertDiagBlocksLowerTriangular" | custom-call | tf_op jit(solution)/shard_map/jit(_cho_solve)/triangular_solve | solution.py:313
  154.5 0.2 convolution_bitcast_fusion.1
  154.7 0.3 convolution_bitcast_fusion
  155.0 5.6 %reshape.60 = bf16[5,64,16,2,64]{4,3,2,1,0:T(2,128)(2,1)} reshape(bf16[5,64,16,128]{3,2,1,0:T(8,128)(2,1)} %get-tuple-element.4) | data formatting | bytes 2621440 | tf_op jit(solution)/shard_map/reshape | solution.py:345
  160.6 2.1 %copy.66 = bf16[5,64,16,2,64]{4,2,0,3,1:T(8,128)(2,1)S(1)} copy(bf16[5,64,16,2,64]{4,3,2,1,0:T(2,128)(2,1)} %reshape.60) | data formatting | bytes 2621440 | tf_op jit(solution)/shard_map/reshape | solution.py:345
  162.8 2.0 %slice.67 = bf16[128,4,64,16]{2,3,1,0:T(8,128)(2,1)} slice(bf16[128,5,64,16]{2,3,1,0:T(8,128)(2,1)S(1)} %bitcast.50), slice={[0:128], [0:4], [0:64], [0:16]} | slice | bytes 2097152 | tf_op jit(solution)/shard_map/slice | solution.py:316
  164.8 5.2 %copy.78 = bf16[128,4,64,16]{0,3,1,2:T(8,128)(2,1)} copy(bf16[128,4,64,16]{2,3,1,0:T(8,128)(2,1)} %slice.67) | data formatting | bytes 2097152
  170.0 1.8 %fusion.10 = f32[128,64,16,1]{0,2,3,1:T(8,128)S(1)} fusion(bf16[128,4,64,16]{0,3,1,2:T(8,128)(2,1)} %copy.78, f32[4,16,16,1]{1,2,0,3:T(8,128)S(1)} %convolution_bitcast_fusion), kind=kOutput, calls=%fused_computation.39 | convolution fusion | flops 100663296 | bytes 1576960 | tf_op jit(solution)/shard_map/rjia,jac->ric/dot_general | solution.py:316
  171.8 1.0 copy.73
  172.8 0.6 bitcast_convert_fusion
  173.4 2.4 %fusion.2 = f32[128,64,16]{1,2,0:T(8,128)S(1)} fusion(f32[4,16,16,1]{1,2,0,3:T(8,128)S(1)} %convolution_bitcast_fusion, f32[128,5,64,16]{2,3,1,0:T(8,128)S(1)} %bitcast_convert_fusion), kind=kOutput, calls=%fused_computation.3 | convolution fusion | flops 101187584 | bytes 8945664 | tf_op jit(solution)/shard_map/rjia,jac->ric/dot_general | solution.py:318
  175.8 0.6 copy.72
  176.4 0.1 convert_subtract_fusion
  176.5 1.0 copy.74
  (8 shorter events, 0.1 us)

commit v2 on v1

--- a/solution.py
+++ b/solution.py
@@ -23,22 +23,23 @@
 def powers_kernel(
     n_space, n_sub, rows, ghost,
     index_ref, list_ref, first_ref, blocks_ref,
-    gram_ref, basis_ref,
-    raw, mats, turn, ext, fresh, up, down, near, low, high, gsend, grecv,
+    gram_ref, nat_ref,
+    basis, lined, tall, perm, raw, mats, turn, ext, fresh, up, down, near, low, high, gsend, grecv,
     load_sem, send_sem, recv_sem, gsend_sem, grecv_sem,
 ):
     p = lax.axis_index("space")
     q = lax.axis_index("sub")
     half = ghost // 2
     pairs = rows // 2
-    rounds_sub, rounds_space = log2(n_sub), log2(n_space)
+    rounds_space = log2(n_space)
     has_low = p > 0
+    flat = BS * NRHS
     has_high = p < n_space - 1
 
     per = rows // CHUNKS
     loads = [
         pltpu.make_async_copy(
-            blocks_ref.at[pl.ds(n * per, per)], raw.at[pl.ds(n * per, per)], load_sem.at[n]
+            blocks_ref.at[:, pl.ds(n * per, per)], raw.at[:, pl.ds(n * per, per)], load_sem.at[n]
         )
         for n in range(CHUNKS)
     ]
@@ -74,7 +75,7 @@
         even, odd = first_ref[2 * m], first_ref[2 * m + 1]
         ext[2 * m] = even
         ext[2 * m + 1] = odd
-        basis_ref[0, m] = jnp.where(left16, even, odd)
+        basis[0, m] = jnp.where(left16, even, odd)
         return carry
 
     lax.fori_loop(0, pairs, own_start, 0)
@@ -139,7 +140,7 @@
                 ext[base + 8 * m + 2 * h + 1] = rows_h[:, 128:]
             return carry
 
-        lax.fori_loop(0, half // 4, body, 0)
+        lax.fori_loop(0, half // 4, body, 0, unroll=8)
 
     def receive(j):
         near_copies, up_copy, down_copy = copies(j)
@@ -164,26 +165,32 @@
         pl.when(has_high)(up_copy.wait_send)
         pl.when(has_low)(down_copy.wait_send)
 
-    def relay(i, carry):
-        for t in range(32):
-            turn[t * 8:t * 8 + NNZ, :] = raw[i, :, t * 128:(t + 1) * 128].astype(jnp.float32)
-        planes = [turn[pl.ds(b, 32, stride=8), :] for b in range(NNZ)]
-        swapped = [pltpu.roll(plane, BS, 1) for plane in planes]
-        zeros = jnp.zeros((32, 128), jnp.float32)
-        planes.append(zeros)
-        swapped.append(zeros)
+    def relay(g, carry):
+        base = pl.multiple_of(g * 16, 16)
         for m in range(4):
-            a, b = 2 * m, 2 * m + 1
-            mats[i, 0:32, m * 128:(m + 1) * 128] = jnp.where(left32, planes[a], swapped[b]).astype(jnp.bfloat16)
-            mats[i, 32:64, m * 128:(m + 1) * 128] = jnp.where(left32, swapped[a], planes[b]).astype(jnp.bfloat16)
+            members = [b for b in (2 * m, 2 * m + 1) if b < NNZ]
+            for b in members:
+                for t in range(32):
+                    turn[b % 2, t * 16:(t + 1) * 16, :] = raw[
+                        b, pl.ds(base, 16), t * 128:(t + 1) * 128
+                    ].astype(jnp.float32)
+            for u in range(16):
+                planes = [turn[b % 2, pl.ds(u, 32, stride=16), :] for b in members]
+                swapped = [pltpu.roll(plane, BS, 1) for plane in planes]
+                if len(members) < 2:
+                    planes.append(jnp.zeros((32, 128), jnp.float32))
+                    swapped.append(planes[1])
+                lanes = slice(m * 128, (m + 1) * 128)
+                mats[base + u, 0:32, lanes] = jnp.where(left32, planes[0], swapped[1]).astype(jnp.bfloat16)
+                mats[base + u, 32:64, lanes] = jnp.where(left32, swapped[0], planes[1]).astype(jnp.bfloat16)
         return carry
 
     def product(j):
         def body(g, carry):
             lines = []
             for u in range(4):
-                at = (4 * g + u) * NNZ
-                tiles = [ext[index_ref[at + b]] for b in range(NNZ)]
+                at = 4 * g + u
+                tiles = [ext[index_ref[b, at]] for b in range(NNZ)]
                 lines.append(jnp.concatenate(
                     [jnp.where(left16, tiles[2 * m], tiles[2 * m + 1]) for m in range(3)] + [tiles[6]], axis=1
                 ))
@@ -207,10 +214,10 @@
                 odd = wide[h * NRHS:(h + 1) * NRHS, 128:]
                 fresh[4 * g + 2 * h] = even
                 fresh[4 * g + 2 * h + 1] = odd
-                basis_ref[j + 1, 2 * g + h] = jnp.where(left16, even, odd)
-            return carry
-
-        lax.fori_loop(0, rows // 4, body, 0)
+                basis[j + 1, 2 * g + h] = jnp.where(left16, even, odd)
+            return carry
+
+        lax.fori_loop(0, rows // 4, body, 0, unroll=4)
 
         def take(m, carry):
             ext[m] = fresh[m]
@@ -219,12 +226,42 @@
         if j < S - 1:
             lax.fori_loop(0, rows, take, 0, unroll=8)
 
+    def natural(j):
+        def line(m, carry):
+            base = pl.multiple_of(m * 32, 32)
+            tall[...] = fresh[pl.ds(base, 32)].reshape(32 * NRHS, 128).astype(jnp.float32)
+            planes = [tall[pl.ds(k, 32, stride=NRHS), :] for k in range(NRHS)]
+            for k in range(NRHS // 2):
+                lined[pl.ds(base, 32), k * 128:(k + 1) * 128] = jnp.where(
+                    left32, planes[2 * k], planes[2 * k + 1]
+                ).astype(jnp.bfloat16)
+            return carry
+
+        lax.fori_loop(0, rows // 32, line, 0)
+        for n in range(flat // 256):
+            lanes = slice(n * 256, (n + 1) * 256)
+            nat_ref[j, :, lanes] = jnp.dot(
+                lined[...], perm[:, lanes], preferred_element_type=jnp.float32
+            ).astype(jnp.bfloat16)
+
+    def permutation(k, carry):
+        at = lax.broadcasted_iota(jnp.int32, (BS, flat), 1)
+        c = lax.broadcasted_iota(jnp.int32, (BS, flat), 0)
+        perm[pl.ds(pl.multiple_of(k * BS, BS), BS), :] = jnp.where(
+            at == c * NRHS + k, 1.0, 0.0
+        ).astype(jnp.bfloat16)
+        return carry
+
     for j in range(S):
         send(j)
+        if j == 1:
+            lax.fori_loop(0, NRHS, permutation, 0)
+        if j >= 1:
+            natural(j - 1)
         if j == 0:
             for n in range(CHUNKS):
                 loads[n].wait()
-                lax.fori_loop(n * per, (n + 1) * per, relay, 0)
+                lax.fori_loop(n * per // 16, (n + 1) * per // 16, relay, 0)
         receive(j)
         product(j)
         sent(j)
@@ -233,44 +270,54 @@
 
     def gram_step(m, total):
         tile = jnp.concatenate(
-            [basis_ref[:, 2 * m + h].reshape(width, 128) for h in range(2)], axis=1
+            [basis[:, 8 * m + h].reshape(width, 128) for h in range(8)], axis=1
         )
         return total + lax.dot_general(tile, tile, NT, preferred_element_type=jnp.float32)
 
-    total = lax.fori_loop(0, pairs // 2, gram_step, jnp.zeros((width, width), jnp.float32))
-    rounds = rounds_sub + rounds_space
+    total = lax.fori_loop(0, pairs // 8, gram_step, jnp.zeros((width, width), jnp.float32), unroll=2)
     gsend[...] = jnp.zeros_like(gsend)
     gsend[0, :, :width] = total
-    for r in range(rounds):
-        if r < rounds_sub:
-            partner = (p, flip(q, 1 << r))
-        else:
-            partner = (flip(p, 1 << (r - rounds_sub)), q)
+    peers = [
+        pltpu.make_async_remote_copy(
+            src_ref=gsend.at[0], dst_ref=grecv.at[d - 1],
+            send_sem=gsend_sem.at[d - 1], recv_sem=grecv_sem.at[d - 1],
+            device_id=(p, (q + d) % n_sub), device_id_type=MESH,
+        )
+        for d in range(1, n_sub)
+    ]
+    for copy in peers:
+        copy.start()
+    natural(S - 1)
+    value = gsend[0]
+    for d, copy in enumerate(peers):
+        copy.wait()
+        value = value + grecv[d]
+    for r in range(rounds_space):
+        at = n_sub - 1 + r
+        gsend[r + 1] = value
         copy = pltpu.make_async_remote_copy(
-            src_ref=gsend.at[r], dst_ref=grecv.at[r],
-            send_sem=gsend_sem.at[r], recv_sem=grecv_sem.at[r],
-            device_id=partner, device_id_type=MESH,
+            src_ref=gsend.at[r + 1], dst_ref=grecv.at[at],
+            send_sem=gsend_sem.at[at], recv_sem=grecv_sem.at[at],
+            device_id=(flip(p, 1 << r), q), device_id_type=MESH,
         )
         copy.start()
         copy.wait()
-        if r < rounds - 1:
-            gsend[r + 1] = gsend[r] + grecv[r]
-        else:
-            gram_ref[...] = gsend[r] + grecv[r]
+        value = value + grecv[at]
+    gram_ref[...] = value
 
 
 def powers(n_space, n_sub, index, lists, first, blocks):
-    rows = blocks.shape[0]
+    rows = blocks.shape[1]
     ghost = lists.shape[0] // 2
     half = ghost // 2
     width = (S + 1) * NRHS
-    rounds = log2(n_sub) + log2(n_space)
+    rounds = n_sub - 1 + log2(n_space)
     bf, f32 = jnp.bfloat16, jnp.float32
     return pl.pallas_call(
         functools.partial(powers_kernel, n_space, n_sub, rows, ghost),
         out_shape=(
             jax.ShapeDtypeStruct((width, 128), f32),
-            jax.ShapeDtypeStruct((S + 1, rows // 2, NRHS, 128), bf),
+            jax.ShapeDtypeStruct((S, rows, BS * NRHS), bf),
         ),
         in_specs=[
             pl.BlockSpec(memory_space=pltpu.SMEM),
@@ -280,9 +327,13 @@
         ],
         out_specs=[pl.BlockSpec(memory_space=pltpu.VMEM)] * 2,
         scratch_shapes=[
-            pltpu.VMEM((rows, NNZ, BS * BS), bf),
+            pltpu.VMEM((S + 1, rows // 2, NRHS, 128), bf),
+            pltpu.VMEM((rows, BS * NRHS), bf),
+            pltpu.VMEM((32 * NRHS, 128), f32),
+            pltpu.VMEM((BS * NRHS, BS * NRHS), bf),
+            pltpu.VMEM((NNZ, rows, BS * BS), bf),
             pltpu.VMEM((rows, BS, 512), bf),
-            pltpu.VMEM((256, 128), f32),
+            pltpu.VMEM((2, 512, 128), f32),
             pltpu.VMEM((rows + n_sub * ghost + 2 * ghost, NRHS, 128), bf),
             pltpu.VMEM((rows, NRHS, 128), bf),
             pltpu.VMEM((S, half, NRHS, 128), bf),
@@ -304,20 +355,60 @@
     )(index, lists, first, blocks)
 
 
-def finish(rhs, stack, gram):
-    rows = stack.shape[0]
-    paired = gram[1:] + gram[:-1]
-    hmat = (paired[:, :, 1:] + paired[:, :, :-1]).reshape(S * NRHS, S * NRHS)
-    cvec = paired[:, :, 0].reshape(S * NRHS, NRHS)
-    lower = jnp.linalg.cholesky(hmat)
-    coef = jax.scipy.linalg.cho_solve((lower, True), cvec).reshape(S, NRHS, NRHS)
-    kfull = stack.astype(jnp.float32)
-    highest = lax.Precision.HIGHEST
-    sol = jnp.einsum("rjia,jac->ric", kfull[:, :S], coef, precision=highest)
-    wmat = kfull[:, 1:] + kfull[:, :S]
-    image = jnp.einsum("rjia,jac->ric", wmat, coef, precision=highest)
-    res = rhs.astype(jnp.float32).reshape(rows, BS, NRHS) - image
-    return (sol.reshape(rows, BS * NRHS), res.reshape(rows, BS * NRHS))
+def split(value):
+    high = value.astype(jnp.bfloat16)
+    rest = value - high.astype(jnp.float32)
+    middle = rest.astype(jnp.bfloat16)
+    return high, middle, (rest - middle.astype(jnp.float32)).astype(jnp.bfloat16)
+
+
+def finish_kernel(gram_ref, rhs_ref, nat_ref, sol_ref, res_ref):
+    size = S * NRHS
+    gram = gram_ref[...]
+    paired = gram[NRHS:] + gram[:size]
+    lane = lax.broadcasted_iota(jnp.int32, (size, 128), 1)
+    row = lax.broadcasted_iota(jnp.int32, (size, 128), 0)
+    work = jnp.where(
+        lane < size, paired + pltpu.roll(paired, 128 - NRHS, 1), pltpu.roll(paired, size, 1)
+    )
+    for k in range(size):
+        line = work[k:k + 1]
+        factor = jnp.where(row[:, :1] == k, 0.0, work[:, k:k + 1] * (1.0 / line[:, k:k + 1]))
+        work = work - factor * line
+    diagonal = jnp.sum(jnp.where(lane == row, work, 0.0), axis=1, keepdims=True)
+    coef = pltpu.roll(work / diagonal, size, 1)
+    coef = jnp.where(lane < NRHS, coef, 0.0)
+    for step in (NRHS, 2 * NRHS, 4 * NRHS):
+        coef = coef + pltpu.roll(coef, step, 1)
+    zero = jnp.zeros((NRHS, 128), jnp.float32)
+    parts = [coef[j * NRHS:(j + 1) * NRHS] for j in range(S)]
+    for_sol = parts + [zero]
+    for_res = [parts[0]] + [parts[j] + parts[j - 1] for j in range(1, S)] + [parts[S - 1]]
+    group = lax.broadcasted_iota(jnp.int32, (128, 256), 0) // NRHS
+    place = (lax.broadcasted_iota(jnp.int32, (128, 256), 1) % 128) // NRHS
+    table = []
+    for j in range(S + 1):
+        both = jnp.concatenate([for_sol[j], for_res[j]], axis=1)
+        table.append(jnp.where(group == place, jnp.concatenate([both] * 8, axis=0), 0.0))
+    tables = split(jnp.concatenate(table, axis=0))
+    for u in range(BS * NRHS // 128):
+        lanes = slice(u * 128, (u + 1) * 128)
+        first = rhs_ref[:, lanes]
+        lhs = jnp.concatenate([first] + [nat_ref[j, :, lanes] for j in range(S)], axis=1)
+        out = sum(jnp.dot(lhs, part, preferred_element_type=jnp.float32) for part in reversed(tables))
+        sol_ref[:, lanes] = out[:, :128]
+        res_ref[:, lanes] = first.astype(jnp.float32) - out[:, 128:]
+
+
+def finish(gram, rhs, nat):
+    shape = jax.ShapeDtypeStruct(rhs.shape, jnp.float32)
+    return pl.pallas_call(
+        finish_kernel,
+        out_shape=(shape, shape),
+        in_specs=[pl.BlockSpec(memory_space=pltpu.VMEM)] * 3,
+        out_specs=[pl.BlockSpec(memory_space=pltpu.VMEM)] * 2,
+        compiler_params=pltpu.CompilerParams(vmem_limit_bytes=24 * 1024 * 1024),
+    )(gram, rhs, nat)
 
 
 def on_device(rhs, blocks, columns, ghost_lists):
@@ -327,23 +418,21 @@
     q = lax.axis_index("sub")
     lists = ghost_lists[0]
     every = lax.all_gather(lists, "sub", axis=0)
-    near = columns[:, 1:3]
+    columns = columns.T
+    near = columns[1:3]
     peer, row = near // rows, near % rows
     owner = jnp.arange(n_sub, dtype=jnp.int32)
     match = (peer[..., None, None] == owner[:, None]) & (row[..., None, None] == every[:, :ghost])
     place = jnp.sum(jnp.where(match, jnp.arange(ghost, dtype=jnp.int32), 0), axis=(2, 3))
     slot = (q - peer - 1) % n_sub
     near = jnp.where(peer == q, row, rows + slot * ghost + place)
-    far = columns[:, 3:] - n_sub * rows + rows + n_sub * ghost
-    local = jnp.arange(rows, dtype=jnp.int32)[:, None]
-    index = jnp.concatenate([local, near, far], axis=1).reshape(-1)
+    far = columns[3:] - n_sub * rows + rows + n_sub * ghost
+    local = jnp.arange(rows, dtype=jnp.int32)[None]
+    index = jnp.concatenate([local, near, far], axis=0)
     first = rhs.reshape(rows, BS, NRHS).transpose(0, 2, 1)
     first = jnp.concatenate([first, first], axis=2)
-    gram, basis = powers(n_space, n_sub, index, lists, first, blocks)
-    width = (S + 1) * NRHS
-    gram = gram[:, :width].reshape(S + 1, NRHS, S + 1, NRHS)
-    stack = basis.reshape(S + 1, rows // 2, NRHS, 2, BS).transpose(1, 3, 0, 4, 2)
-    return finish(rhs, stack.reshape(rows, S + 1, BS, NRHS), gram)
+    gram, nat = powers(n_space, n_sub, index, lists, first, blocks.transpose(1, 0, 2))
+    return finish(gram, rhs, nat)
 
 
 def solution(mesh):

time: 178 us -> 112 us (0.63)
  local copies, waits for them, and re-layouts: 31 us -> 3.66 us
  Pallas kernels: 119 us -> 98 us
  other arithmetic: 16.2 us -> 3.28 us
  matrix products: 4.73 us -> 0 us
    pallas_call x1, Pallas kernels: 119 us -> 89.8 us  [powers(): pl.pallas_call(functools.partial(powers_kernel, n_space, n_sub, rows, gho...]
    unnamed x5 -> x7, local copies, waits for them, and re-layouts: 18.7 us -> 3.12 us
    another operation x5 -> x0, other arithmetic: 12.1 us -> none  [the longest x3 6.52 us: finish(): lower = jnp.linalg.cholesky(hmat)]
    reshape x5 -> x0, local copies, waits for them, and re-layouts: 8.74 us -> none  [the longest x2 7.75 us: on_device(): basis.reshape(S + 1, rows // 2, NRHS, 2, BS).transpose(1, 3, 0, 4, 2)]
    pallas_call x0 -> x1, Pallas kernels: none -> 8.21 us  [finish(): pl.pallas_call(finish_kernel, out_shape=(shape, shape), in_specs=[pl.Bloc...]
    dot_general x2 -> x0, matrix products: 4.24 us -> none  [the longest x1 2.43 us: finish(): image = jnp.einsum('rjia,jac->ric', wmat, coef, precision=highest)]
    slice x2 -> x0, local copies, waits for them, and re-layouts: 2.01 us -> none  [the longest x1 2.01 us: finish(): sol = jnp.einsum('rjia,jac->ric', kfull[:, :S], coef, precision=highest)]
where the time goes in v2:
time: 112 us
  Pallas kernels  98 us (88%)
  blocking collectives  6.13 us (5%)
  local copies, waits for them, and re-layouts  3.66 us (3%)
  other arithmetic  3.28 us (3%)
    pallas_call x1, Pallas kernels, powers(): pl.pallas_call(functools.partial(powers_kernel, n_space, n_sub, rows, gho...  89.8 us
    pallas_call x1, Pallas kernels, finish(): pl.pallas_call(finish_kernel, out_shape=(shape, shape), in_specs=[pl.Bloc...  8.21 us
    all_gather x1, blocking collectives, on_device(): every = lax.all_gather(lists, 'sub', axis=0)  6.13 us
    unnamed x7, local copies, waits for them, and re-layouts  3.12 us

profile of v2, /device:TPU:0, one launch (start us, length us, event | category | flops | bytes accessed | tf_op | source)
XLA Modules:
  0.0 111.8 jit_solution(5204051886068227358)
XLA Ops:
  0.6 0.0 copy-start.1
  0.7 0.7 slice_add_fusion
  1.4 6.1 %all-gather = s32[4,1,128]{2,1,0:T(1,128)S(1)} all-gather(s32[1,1,128]{2,1,0:T(1,128)} %bitcast.14), channel_id=1, replica_groups=mesh['space'=8,'sub'=4] {'sub'}, dimensions={0}, use_global_device_ids=true | all-gather | bytes 2560 | tf_op jit(solution)/shard_map/all_gather | solution.py:420
  7.5 0.7 and_select_fusion.2
  8.2 0.1 select_reduce_fusion
  8.4 0.6 pad_add_fusion.index_ref
  9.0 1.1 copy.10
  10.1 0.5 copy.11
  10.7 1.1 pad_maximum_fusion.first_ref
  11.7 89.8 %shard_map.59 = (f32[80,128]{1,0:T(8,128)}, bf16[4,128,1024]{2,1,0:T(8,128)(2,1)}) custom-call(s32[7,128]{1,0:T(8,128)} %pad_add_fusion.index_ref, s32[128]{0:T(128)} %bitcast.15, bf16[128,16,128]{2,1,0:T(8,128)(2,1)} %pad_maximum_fusion.first_ref, bf16[7,128,4096]{2,1,0:T(8,128)(2,1)} %bitcast.8), custom_call_target="tpu_custom_call" | custom-call | tf_op jit(solution)/shard_map/pallas_call | solution.py:316
  101.5 0.0 copy-done.1
  101.5 0.0 copy-start
  101.5 1.2 %copy-done = bf16[4,128,1024]{2,1,0:T(8,128)(2,1)S(1)} copy-done((bf16[4,128,1024]{2,1,0:T(8,128)(2,1)S(1)}, bf16[4,128,1024]{2,1,0:T(8,128)(2,1)}, u32[]{:S(2)}) %copy-start) | copy-done | bytes 1048600
  102.8 0.0 copy-start.2
  102.8 0.8 copy-done.2
  103.5 8.2 %shard_map.60 = (f32[128,1024]{1,0:T(8,128)}, f32[128,1024]{1,0:T(8,128)}) custom-call(f32[80,128]{1,0:T(8,128)S(1)} %copy-done.2, bf16[128,1024]{1,0:T(8,128)(2,1)S(1)} %copy-done.1, bf16[4,128,1024]{2,1,0:T(8,128)(2,1)S(1)} %copy-done), custom_call_target="tpu_custom_call" | custom-call | tf_op jit(solution)/shard_map/pallas_call | solution.py:405
  (3 shorter events, 0.0 us)
Async XLA Ops:
  0.6 100.9 %copy-start.1 = (bf16[128,1024]{1,0:T(8,128)(2,1)S(1)}, bf16[128,1024]{1,0:T(8,128)(2,1)}, u32[]{:S(2)}) copy-start(bf16[128,1024]{1,0:T(8,128)(2,1)} %rhs_ref.1) | copy-start | bytes 786436
  101.5 1.2 %copy-start = (bf16[4,128,1024]{2,1,0:T(8,128)(2,1)S(1)}, bf16[4,128,1024]{2,1,0:T(8,128)(2,1)}, u32[]{:S(2)}) copy-start(bf16[4,128,1024]{2,1,0:T(8,128)(2,1)} %get-tuple-element.5.nat_ref) | copy-start | bytes 3145732
  102.8 0.8 copy-start.2

commit v3 on v2

--- a/solution.py
+++ b/solution.py
@@ -14,6 +14,8 @@
 MESH = pl.DeviceIdType.MESH
 NT = (((1,), (1,)), ((), ()))
 CHUNKS = 4
+BATCH = 32
+PACK = 16
 
 
 def log2(n):
@@ -110,37 +112,38 @@
     def send(j):
         near_copies, up_copy, down_copy = copies(j)
 
-        def pack_up(m, carry):
-            up[j, m] = jnp.where(left16, ext[list_ref[2 * m]], ext[list_ref[2 * m + 1]])
-            return carry
-
-        def pack_down(m, carry):
-            down[j, m] = jnp.where(
-                left16, ext[list_ref[ghost + 2 * m]], ext[list_ref[ghost + 2 * m + 1]]
-            )
-            return carry
-
-        lax.fori_loop(0, half, pack_up, 0, unroll=4)
+        def pack(target, start):
+            def body(m, carry):
+                taken = [
+                    jnp.where(
+                        left16,
+                        ext[list_ref[start + 2 * (PACK * m + u)]],
+                        ext[list_ref[start + 2 * (PACK * m + u) + 1]],
+                    )
+                    for u in range(PACK)
+                ]
+                for u in range(PACK):
+                    target[j, PACK * m + u] = taken[u]
+                return carry
+
+            lax.fori_loop(0, half // PACK, body, 0)
+
+        pack(up, 0)
         if j == 0:
             greeted = (n_sub - 1) + (rounds_space - 1)
             pl.semaphore_wait(barrier, greeted + jnp.where(has_low, 1, 0) + jnp.where(has_high, 1, 0))
         pl.when(has_high)(up_copy.start)
         for copy in near_copies:
             copy.start()
-        lax.fori_loop(0, half, pack_down, 0, unroll=4)
+        pack(down, ghost)
         pl.when(has_low)(down_copy.start)
 
     def spread(buffer, lead, base):
-        def body(m, carry):
-            part = buffer[lead + (pl.ds(4 * m, 4),)].reshape(4 * NRHS, 128)
-            wide = jnp.dot(part, double, preferred_element_type=jnp.float32).astype(jnp.bfloat16)
-            for h in range(4):
-                rows_h = wide[h * NRHS:(h + 1) * NRHS]
-                ext[base + 8 * m + 2 * h] = rows_h[:, :128]
-                ext[base + 8 * m + 2 * h + 1] = rows_h[:, 128:]
-            return carry
-
-        lax.fori_loop(0, half // 4, body, 0, unroll=8)
+        part = buffer[lead].reshape(half * NRHS, 128)
+        wide = jnp.dot(part, double, preferred_element_type=jnp.float32).astype(jnp.bfloat16)
+        for h in range(half):
+            ext[base + 2 * h] = wide[h * NRHS:(h + 1) * NRHS, :128]
+            ext[base + 2 * h + 1] = wide[h * NRHS:(h + 1) * NRHS, 128:]
 
     def receive(j):
         near_copies, up_copy, down_copy = copies(j)
@@ -185,46 +188,44 @@
                 mats[base + u, 32:64, lanes] = jnp.where(left32, swapped[0], planes[1]).astype(jnp.bfloat16)
         return carry
 
+    def picks(at, count):
+        lines = []
+        for u in range(count):
+            tiles = [ext[index_ref[b, at + u]] for b in range(NNZ)]
+            lines.append(jnp.concatenate(
+                [jnp.where(left16, tiles[2 * m], tiles[2 * m + 1]) for m in range(3)] + [tiles[6]], axis=1
+            ))
+        return jnp.concatenate(lines, axis=0)
+
     def product(j):
         def body(g, carry):
-            lines = []
-            for u in range(4):
-                at = 4 * g + u
-                tiles = [ext[index_ref[b, at]] for b in range(NNZ)]
-                lines.append(jnp.concatenate(
-                    [jnp.where(left16, tiles[2 * m], tiles[2 * m + 1]) for m in range(3)] + [tiles[6]], axis=1
-                ))
-            lhs = jnp.concatenate(lines, axis=0)
-            rhs = mats[pl.ds(4 * g, 4)].reshape(4 * BS, 512)
-            full = lax.dot_general(lhs, rhs, NT, preferred_element_type=jnp.float32)
-            left = left16
-            picked = [
-                jnp.where(
-                    left,
-                    full[2 * h * NRHS:(2 * h + 1) * NRHS, h * 128:(h + 1) * 128],
-                    full[(2 * h + 1) * NRHS:(2 * h + 2) * NRHS, h * 128:(h + 1) * 128],
-                ).astype(jnp.bfloat16)
-                for h in range(2)
-            ]
+            start = BATCH * g
+            lhs = [picks(start + 4 * n, 4) for n in range(BATCH // 4)]
+            picked = []
+            for n in range(BATCH // 4):
+                block = mats[pl.ds(start + 4 * n, 4)].reshape(4 * BS, 512)
+                full = lax.dot_general(lhs[n], block, NT, preferred_element_type=jnp.float32)
+                for h in range(2):
+                    picked.append(jnp.where(
+                        left16,
+                        full[2 * h * NRHS:(2 * h + 1) * NRHS, h * 128:(h + 1) * 128],
+                        full[(2 * h + 1) * NRHS:(2 * h + 2) * NRHS, h * 128:(h + 1) * 128],
+                    ).astype(jnp.bfloat16))
             wide = jnp.dot(
                 jnp.concatenate(picked, axis=0), order, preferred_element_type=jnp.float32
             ).astype(jnp.bfloat16)
-            for h in range(2):
+            for h in range(BATCH // 2):
                 even = wide[h * NRHS:(h + 1) * NRHS, :128]
                 odd = wide[h * NRHS:(h + 1) * NRHS, 128:]
-                fresh[4 * g + 2 * h] = even
-                fresh[4 * g + 2 * h + 1] = odd
-                basis[j + 1, 2 * g + h] = jnp.where(left16, even, odd)
+                fresh[start + 2 * h] = even
+                fresh[start + 2 * h + 1] = odd
+                basis[j + 1, BATCH // 2 * g + h] = jnp.where(left16, even, odd)
             return carry
 
-        lax.fori_loop(0, rows // 4, body, 0, unroll=4)
-
-        def take(m, carry):
-            ext[m] = fresh[m]
-            return carry
+        lax.fori_loop(0, rows // BATCH, body, 0)
 
         if j < S - 1:
-            lax.fori_loop(0, rows, take, 0, unroll=8)
+            ext[pl.ds(0, rows)] = fresh[...]
 
     def natural(j):
         def line(m, carry):

time: 112 us -> 89.3 us (0.80)
  Pallas kernels: 98 us -> 75.2 us
    pallas_call x1, Pallas kernels: 89.8 us -> 67 us  [powers(): pl.pallas_call(functools.partial(powers_kernel, n_space, n_sub, rows, gho...]
where the time goes in v3:
time: 89.3 us; the launch traced here: 88.9 us
  Pallas kernels  75.2 us (84%)
  blocking collectives  6.13 us (7%)
  local copies, waits for them, and re-layouts  3.66 us (4%)
  other arithmetic  3.28 us (4%)
    pallas_call x1, Pallas kernels, powers(): pl.pallas_call(functools.partial(powers_kernel, n_space, n_sub, rows, gho...  67 us
    pallas_call x1, Pallas kernels, finish(): pl.pallas_call(finish_kernel, out_shape=(shape, shape), in_specs=[pl.Bloc...  8.21 us
    all_gather x1, blocking collectives, on_device(): every = lax.all_gather(lists, 'sub', axis=0)  6.13 us
    unnamed x7, local copies, waits for them, and re-layouts  3.12 us

profile of v3, /device:TPU:0, one launch (start us, length us, event | category | flops | bytes accessed | tf_op | source)
XLA Modules:
  0.0 88.9 jit_solution(12366460676554937748)
XLA Ops:
  0.6 0.0 copy-start.1
  0.7 0.7 slice_add_fusion
  1.4 6.1 %all-gather = s32[4,1,128]{2,1,0:T(1,128)S(1)} all-gather(s32[1,1,128]{2,1,0:T(1,128)} %bitcast.14), channel_id=1, replica_groups=mesh['space'=8,'sub'=4] {'sub'}, dimensions={0}, use_global_device_ids=true | all-gather | bytes 2560 | tf_op jit(solution)/shard_map/all_gather | solution.py:421
  7.5 0.7 and_select_fusion.2
  8.2 0.1 select_reduce_fusion
  8.4 0.6 pad_add_fusion.index_ref
  9.0 1.1 %copy.10 = bf16[128,1024]{0,1:T(8,128)(2,1)S(1)} copy(bf16[128,1024]{1,0:T(8,128)(2,1)} %rhs_ref.1) | data formatting | bytes 524288 | tf_op args[0]
  10.1 0.5 copy.11
  10.7 1.1 %pad_maximum_fusion.first_ref = bf16[128,16,128]{2,1,0:T(8,128)(2,1)} fusion(bf16[128,16,64]{2,1,0:T(8,128)(2,1)S(1)} %bitcast.9), kind=kLoop, calls=%fused_computation | loop fusion | flops 1048576 | bytes 786432 | tf_op jit(solution)/shard_map/concatenate | solution.py:434
  11.7 67.0 %shard_map.59 = (f32[80,128]{1,0:T(8,128)}, bf16[4,128,1024]{2,1,0:T(8,128)(2,1)}) custom-call(s32[7,128]{1,0:T(8,128)} %pad_add_fusion.index_ref, s32[128]{0:T(128)} %bitcast.15, bf16[128,16,128]{2,1,0:T(8,128)(2,1)} %pad_maximum_fusion.first_ref, bf16[7,128,4096]{2,1,0:T(8,128)(2,1)} %bitcast.8), custom_call_target="tpu_custom_call" | custom-call | tf_op jit(solution)/shard_map/pallas_call | solution.py:317
  78.7 0.0 copy-done.1
  78.7 0.0 copy-start
  78.7 1.2 %copy-done = bf16[4,128,1024]{2,1,0:T(8,128)(2,1)S(1)} copy-done((bf16[4,128,1024]{2,1,0:T(8,128)(2,1)S(1)}, bf16[4,128,1024]{2,1,0:T(8,128)(2,1)}, u32[]{:S(2)}) %copy-start) | copy-done | bytes 1048600
  79.9 0.0 copy-start.2
  80.0 0.8 copy-done.2
  80.7 8.2 %shard_map.60 = (f32[128,1024]{1,0:T(8,128)}, f32[128,1024]{1,0:T(8,128)}) custom-call(f32[80,128]{1,0:T(8,128)S(1)} %copy-done.2, bf16[128,1024]{1,0:T(8,128)(2,1)S(1)} %copy-done.1, bf16[4,128,1024]{2,1,0:T(8,128)(2,1)S(1)} %copy-done), custom_call_target="tpu_custom_call" | custom-call | tf_op jit(solution)/shard_map/pallas_call | solution.py:406
  (3 shorter events, 0.0 us)
Async XLA Ops:
  0.6 78.1 %copy-start.1 = (bf16[128,1024]{1,0:T(8,128)(2,1)S(1)}, bf16[128,1024]{1,0:T(8,128)(2,1)}, u32[]{:S(2)}) copy-start(bf16[128,1024]{1,0:T(8,128)(2,1)} %rhs_ref.1) | copy-start | bytes 786436
  78.7 1.2 %copy-start = (bf16[4,128,1024]{2,1,0:T(8,128)(2,1)S(1)}, bf16[4,128,1024]{2,1,0:T(8,128)(2,1)}, u32[]{:S(2)}) copy-start(bf16[4,128,1024]{2,1,0:T(8,128)(2,1)} %get-tuple-element.5.nat_ref) | copy-start | bytes 3145732
  79.9 0.8 copy-start.2
